TPU v7x, 32 devices: a whole 2x2x4 slice. The times are simulated.
32 devices in a mesh: parts: 2 (over x), lat: 16 (over z, y, core).
Axes of the slice: x: 2, y: 2, z: 4, core: 2. Of those that a mesh axis runs over, the one named last changes fastest.
Arguments:
- grid_field: float32 [368, 1440, 256], P('lat', None, 'parts'), parts along dimension 2, may hold values from -170 to 170
- norm_gain: float32 [128], P('parts'), parts along dimension 0, may hold values from 0.5 to 1.5
- filter_weight: bfloat16 [352, 2, 64, 128], P('lat', None, None, 'parts'), parts along dimension 3, may hold values from -0.5 to 0.5
Outputs:
- spectrum_out: bfloat16 [352, 352, 512], P('lat', None, 'parts'), parts along dimension 2
There are 2 independent parts, one for each index of `parts`. A program takes and returns all parts, laid end to end along the dimension named above; each array names one. Nothing has to cross between parts.
All inputs are finite; a program needn't handle non-finite values.
Results may differ from a plain program's by a relative error of at most 0.0064.
Values may be sent and summed in bfloat16 or wider, within the bound.
A program may use at most 192 MiB of HBM per device.

v0:
```python
import math
import jax
import jax.numpy as jnp
from jax import lax
from jax.sharding import PartitionSpec as P

C = 64
S = 2
DEG_DEV = 22


def legendre_table(colatitude, orders, degrees, weight_scale):
    cosine = jnp.cos(colatitude)[:, None]
    sine_rows = jnp.sin(colatitude)
    order_sq = orders * orders
    log_start = 0.5 * jnp.log((2.0 * orders + 1.0) / (4.0 * math.pi)) + 0.5 * (
        lax.lgamma(orders + 0.5) - lax.lgamma(orders + 1.0) - 0.5 * math.log(math.pi)
    )
    log_diag = log_start[None, :] + orders[None, :] * jnp.log(sine_rows)[:, None]
    start_exp = 64.0 * jnp.floor(log_diag / (64.0 * math.log(2.0)))
    start_mant = jnp.exp(log_diag - start_exp * math.log(2.0))
    weights = (weight_scale * sine_rows)[:, None]
    limit = 2.0**64
    shrink = 2.0 ** (-64)

    def recurrence(state, degree):
        previous, earlier, exponent = state
        degree_value = degree.astype(orders.dtype)
        upper_coef = jnp.sqrt(
            (4.0 * degree_value * degree_value - 1.0)
            / jnp.maximum(degree_value * degree_value - order_sq, 1.0)
        )
        below = degree_value - 1.0
        lower_coef = jnp.sqrt(
            jnp.maximum(below * below - order_sq, 0.0) / jnp.maximum(4.0 * below * below - 1.0, 1.0)
        )
        recurred = upper_coef * (cosine * previous - lower_coef * earlier)
        at_start = degree_value == orders
        current = jnp.where(at_start, start_mant, jnp.where(degree_value > orders, recurred, 0.0))
        exponent = jnp.where(at_start, start_exp, exponent)
        value = (weights * (current * jnp.exp2(exponent))).astype(jnp.bfloat16)
        large = jnp.abs(current) > limit
        current = jnp.where(large, current * shrink, current)
        kept = jnp.where(large, previous * shrink, previous)
        exponent = jnp.where(large, exponent + 64.0, exponent)
        return ((current, kept, exponent), value)

    zero_state = jnp.zeros((colatitude.shape[0], orders.shape[0]), colatitude.dtype)
    last_state, stacked = lax.scan(
        recurrence,
        (zero_state, zero_state, zero_state),
        jnp.arange(degrees, dtype=jnp.int32),
        unroll=8,
    )
    return stacked


def expand_filter(filter_weight):
    real_part = filter_weight[:, 0]
    imag_part = filter_weight[:, 1]
    from_real = jnp.stack([real_part, imag_part], axis=2)
    from_imag = jnp.stack([-imag_part, real_part], axis=2)
    return jnp.stack([from_real, from_imag], axis=1)


def apply_filter(coefficients, expanded):
    shaped = coefficients.reshape(coefficients.shape[0], coefficients.shape[1], 2, S, C)
    mixed = jnp.einsum("lmrsc,lrcqo->lmqso", shaped, expanded, preferred_element_type=jnp.float32)
    return mixed.astype(jnp.bfloat16).reshape(
        coefficients.shape[0], coefficients.shape[1], 2 * S * C
    )


def moments(grid_field, sine_own, sine_total):
    first_moment = jnp.einsum("j,jnx->x", sine_own, grid_field, precision=lax.Precision.HIGHEST)
    second_moment = jnp.einsum(
        "j,jnx->x", sine_own, grid_field * grid_field, precision=lax.Precision.HIGHEST
    )
    first_moment, second_moment = lax.psum((first_moment, second_moment), "lat")
    denominator = grid_field.shape[1] * sine_total
    average = first_moment / denominator
    second_moment = second_moment / denominator
    spread = jnp.sqrt(second_moment - average * average + 1e-05)
    return (average, spread)


def fourier_sums(fourier_table, grid_data):
    return jnp.einsum("rmn,jnx->jmrx", fourier_table, grid_data, precision=lax.Precision.HIGHEST)


def body(grid_field, norm_gain, filter_weight):
    device_index = lax.axis_index("lat")
    lat_count = lax.axis_size("lat")
    band_rows = grid_field.shape[0]
    longitudes = grid_field.shape[1]
    columns = grid_field.shape[2]
    total_lat = band_rows * lat_count
    order_count = DEG_DEV * lat_count
    all_rows = jnp.arange(total_lat, dtype=jnp.int32)
    colat_all = math.pi * (all_rows.astype(jnp.float32) + 0.5) / total_lat
    sine_total = jnp.sum(jnp.sin(colat_all))
    own_rows = device_index * band_rows + jnp.arange(band_rows, dtype=jnp.int32)
    colat_own = math.pi * (own_rows.astype(jnp.float32) + 0.5) / total_lat
    sine_own = jnp.sin(colat_own)
    order_ints = jnp.arange(order_count, dtype=jnp.int32)
    lon_ints = jnp.arange(longitudes, dtype=jnp.int32)
    phases = order_ints[:, None] * lon_ints[None, :] % longitudes
    angles = 2.0 * math.pi * phases.astype(jnp.float32) / longitudes
    fourier_table = jnp.stack([jnp.cos(angles), -jnp.sin(angles)], axis=0)
    average, spread = moments(grid_field, sine_own, sine_total)
    factor = jnp.tile(norm_gain, S) / spread
    normalized = (grid_field - average) * factor
    spectral = fourier_sums(fourier_table, normalized)
    fourier = spectral.astype(jnp.bfloat16).reshape(band_rows, order_count, 2 * columns)
    weight_scale = math.pi**1.5 / math.sqrt(total_lat * longitudes)
    expanded = expand_filter(filter_weight)
    orders = (device_index * DEG_DEV + jnp.arange(DEG_DEV, dtype=jnp.int32)).astype(jnp.float32)
    legendre = legendre_table(colat_all, orders, order_count, weight_scale)
    order_coefs = jnp.einsum(
        "ljm,jmx->lmx",
        legendre,
        lax.all_to_all(fourier, "lat", split_axis=1, concat_axis=0, tiled=True),
        preferred_element_type=jnp.float32,
    )
    coefficients = lax.all_to_all(
        order_coefs.astype(jnp.bfloat16), "lat", split_axis=0, concat_axis=1, tiled=True
    )
    return apply_filter(coefficients, expanded)


def solution(mesh):
    in_specs = (P("lat", None, "parts"), P("parts"), P("lat", None, None, "parts"))
    out_specs = P("lat", None, "parts")
    return jax.shard_map(body, mesh=mesh, in_specs=in_specs, out_specs=out_specs, check_vma=False)
```

profile of v0, /device:TPU:15, one launch (start us, length us, event | category | flops | bytes accessed | tf_op | source)
XLA Modules:
  0.0 617.7 jit_solution(4828571565384696489)
XLA Ops:
  0.7 9.8 %sine_negate_fusion = (f32[1,352,1440]{2,1,0:T(8,128)S(1)}, f32[1,352,1440]{2,1,0:T(8,128)}) fusion(), kind=kLoop, calls=%fused_computation.172 | loop fusion | flops 5068800 | bytes 4055040 | tf_op jit(solution)/shard_map/neg | solution.py:109
  10.5 7.5 %multiply_reduce_fusion.1 = (f32[23,128]{1,0:T(8,128)S(1)}, f32[23,128]{1,0:T(8,128)S(1)}) fusion(f32[23,1440,128]{2,1,0:T(8,128)} %param.5), kind=kLoop, calls=%fused_computation.155 | loop fusion | flops 12712192 | bytes 16980992 | tf_op jit(solution)/shard_map/j,jnx->x/reduce_sum | solution.py:76
  18.5 21.9 %all-reduce = (f32[128]{0:T(128)S(1)}, f32[128]{0:T(128)S(1)}) all-reduce(f32[128]{0:T(128)S(1)} %convolution_bitcast_fusion.1, f32[128]{0:T(128)S(1)} %convolution_bitcast_fusion), channel_id=1, replica_groups=mesh['parts'=2,'lat'=16] {'lat'}, use_global_device_ids=true, to_apply=%region_1.2 | all-reduce | flops 256 | bytes 2048 | tf_op jit(solution)/shard_map/psum | solution.py:79
  41.0 46.7 %convert_bitcast_fusion = bf16[23,352,2,128]{3,1,2,0:T(8,128)(2,1)S(1)} fusion(f32[1,352,1440]{2,1,0:T(8,128)S(1)} %get-tuple-element.513, f32[1,352,1440]{2,1,0:T(8,128)} %get-tuple-element.514, f32[23,1440,128]{2,1,0:T(8,128)} %param.5, f32[128]{0:T(128)S(1)} %get-tuple-element.464, f32[128]{0:T(128)S(1)} %get-tuple-element.465), kind=kOutput, calls=%fused_computation.167 | convolution fusion | flops 35825680384 | bytes 25158656 | tf_op jit(solution)/shard_map/rmn,jnx->jmrx/dot_general | solution.py:88
  87.7 5.1 copy.35
  92.8 7.6 %reshape.396 = bf16[23,352,256]{2,0,1:T(8,128)(2,1)} reshape(bf16[23,352,2,128]{3,2,0,1:T(2,128)(2,1)} %copy.35) | data formatting | bytes 8290304 | tf_op jit(solution)/shard_map/reshape | solution.py:114
  100.4 16.8 %all-to-all-start = ((bf16[23,352,256]{2,0,1:T(8,128)(2,1)}), bf16[23,352,256]{2,0,1:T(8,128)(2,1)}, u32[]{:S(2)}, u32[]{:S(2)}) async-start(bf16[23,352,256]{2,0,1:T(8,128)(2,1)} %reshape.396), calls=%async_computation | async-start | bytes 8650752 | tf_op jit(solution)/shard_map/all_to_all | solution.py:122
  117.4 342.9 %while.23 = (s32[]{:T(128)}, f32[368,22]{0,1:T(8,128)S(1)}, f32[368,22]{0,1:T(8,128)S(1)}, f32[368,22]{0,1:T(8,128)S(1)}, bf16[44,8,368,22]{2,3,1,0:T(8,128)(2,1...) while((s32[]{:T(128)}, f32[368,22]{0,1:T(8,128)S(1)}, ...), condition=%wide.region_6.7_spmd.clone.clone.clone.clone, body=%wide.region_5.6_spmd.clone.clone.clone.clone.sunk | while | flops 2134202 | bytes 2012586 | solution.py:49
  124.5 0.7 bitcast_dynamic-update-slice_fusion.2
  140.0 0.7 bitcast_dynamic-update-slice_fusion.2
  147.8 0.7 bitcast_dynamic-update-slice_fusion.2
  155.6 0.7 bitcast_dynamic-update-slice_fusion.2
  179.0 0.7 bitcast_dynamic-update-slice_fusion.2
  194.6 0.7 bitcast_dynamic-update-slice_fusion.2
  202.4 0.7 bitcast_dynamic-update-slice_fusion.2
  217.9 0.7 bitcast_dynamic-update-slice_fusion.2
  233.5 0.7 bitcast_dynamic-update-slice_fusion.2
  249.1 0.7 bitcast_dynamic-update-slice_fusion.2
  264.7 0.7 bitcast_dynamic-update-slice_fusion.2
  272.5 0.7 bitcast_dynamic-update-slice_fusion.2
  280.3 0.7 bitcast_dynamic-update-slice_fusion.2
  288.1 0.7 bitcast_dynamic-update-slice_fusion.2
  303.6 0.7 bitcast_dynamic-update-slice_fusion.2
  319.2 0.7 bitcast_dynamic-update-slice_fusion.2
  342.6 0.7 bitcast_dynamic-update-slice_fusion.2
  350.4 0.7 bitcast_dynamic-update-slice_fusion.2
  366.0 0.7 bitcast_dynamic-update-slice_fusion.2
  373.8 0.7 bitcast_dynamic-update-slice_fusion.2
  381.6 0.7 bitcast_dynamic-update-slice_fusion.2
  389.4 0.7 bitcast_dynamic-update-slice_fusion.2
  397.2 0.7 bitcast_dynamic-update-slice_fusion.2
  405.0 0.7 bitcast_dynamic-update-slice_fusion.2
  412.8 0.7 bitcast_dynamic-update-slice_fusion.2
  420.6 0.7 bitcast_dynamic-update-slice_fusion.2
  428.4 0.7 bitcast_dynamic-update-slice_fusion.2
  443.9 0.7 bitcast_dynamic-update-slice_fusion.2
  451.7 0.7 bitcast_dynamic-update-slice_fusion.2
  459.5 0.7 bitcast_dynamic-update-slice_fusion.2
  460.3 4.8 copy.24
  465.1 7.0 %all_to_all.27 = bf16[368,22,256]{2,0,1:T(8,128)(2,1)} reshape(bf16[16,23,22,256]{3,1,0,2:T(8,128)(2,1)} %copy.24) | data formatting | bytes 8290304 | tf_op jit(solution)/shard_map/all_to_all | solution.py:122
  472.1 6.3 %convert_bitcast_fusion.1 = bf16[352,22,256]{2,0,1:T(8,128)(2,1)S(1)} fusion(bf16[368,22,256]{2,0,1:T(8,128)(2,1)} %all_to_all.27, bf16[352,368,22]{1,2,0:T(8,128)(2,1)} %bitcast.140), kind=kOutput, calls=%fused_computation.168 | convolution fusion | flops 1461075968 | bytes 13809664 | tf_op jit(solution)/shard_map/ljm,jmx->lmx/dot_general | solution.py:119
  478.4 4.4 copy.26
  482.7 6.2 %all-to-all-start.1 = ((bf16[352,22,256]{2,1,0:T(8,128)(2,1)}), bf16[352,22,256]{2,1,0:T(8,128)(2,1)}, u32[]{:S(2)}, u32[]{:S(2)}) async-start(bf16[352,22,256]{2,1,0:T(8,128)(2,1)} %copy.26), calls=%async_computation.1 | async-start | bytes 8650752 | tf_op jit(solution)/shard_map/all_to_all | solution.py:125
  489.8 94.4 %all-to-all-done.1 = bf16[352,22,256]{2,1,0:T(8,128)(2,1)} async-done(((bf16[352,22,256]{2,1,0:T(8,128)(2,1)}), bf16[352,22,256]{2,1,0:T(8,128)(2,1)}, u32[]{:S(2)}, u32[]{:S(2)}) %all-to-all-start.1) | async-done | bytes 3964960 | tf_op jit(solution)/shard_map/all_to_all | solution.py:125
  584.2 4.7 copy.28
  589.0 14.4 %reshape.385 = bf16[22,352,2,2,64]{4,3,2,1,0:T(2,128)(2,1)} reshape(bf16[22,16,22,256]{3,2,1,0:T(8,128)(2,1)} %copy.28) | data formatting | bytes 7929856 | tf_op jit(solution)/shard_map/reshape | solution.py:67
  603.3 8.0 %bitcast_convert_fusion = bf16[22,2,64,352,2]{3,2,4,1,0:T(8,128)(2,1)} fusion(bf16[22,352,2,2,64,1]{4,3,2,1,0,5:T(2,128)(2,1)} %bitcast.136, bf16[22,1,64,2,64]{2,4,1,3,0:T(8,128)(2,1)S(1)} %get-tuple-element.512, bf16[22,1,64,2,64]{2,4,1,3,0:T(8,128)(2,1)S(1)} %get-tuple-element.511), kind=kOutput, calls=%fused_computation.157 | convolution fusion | flops 510935040 | bytes 8650752 | tf_op jit(solution)/shard_map/lmrsc,lrcqo->lmqso/dot_general | solution.py:68
  611.4 6.3 %copy.30 = bf16[22,352,256]{2,1,0:T(8,128)(2,1)} copy(bf16[22,352,256]{1,2,0:T(8,128)(2,1)} %bitcast.137) | data formatting | bytes 7929856 | tf_op jit(solution)/shard_map/reshape | solution.py:69
  (1314 shorter events, 99.2 us)
Async XLA Ops:
  10.5 7.9 %copy-start.1 = (f32[64]{0:T(128)S(1)}, f32[64]{0:T(128)}, u32[]{:S(2)}) copy-start(f32[64]{0:T(128)} %param.6) | copy-start | bytes 772
  100.4 359.8 %all-to-all-start = ((bf16[23,352,256]{2,0,1:T(8,128)(2,1)}), bf16[23,352,256]{2,0,1:T(8,128)(2,1)}, u32[]{:S(2)}, u32[]{:S(2)}) async-start(bf16[23,352,256]{2,0,1:T(8,128)(2,1)} %reshape.396), calls=%async_computation | async-start | bytes 8650752 | tf_op jit(solution)/shard_map/all_to_all | solution.py:122
  482.7 6.2 %copy-start = (bf16[22,2,64,64]{3,2,1,0:T(8,128)(2,1)S(1)}, bf16[22,2,64,64]{3,2,1,0:T(8,128)(2,1)}, u32[]{:S(2)}) copy-start(bf16[22,2,64,64]{3,2,1,0:T(8,128)(2,1)} %param.7) | copy-start | bytes 1081348
  482.7 101.5 %all-to-all-start.1 = ((bf16[352,22,256]{2,1,0:T(8,128)(2,1)}), bf16[352,22,256]{2,1,0:T(8,128)(2,1)}, u32[]{:S(2)}, u32[]{:S(2)}) async-start(bf16[352,22,256]{2,1,0:T(8,128)(2,1)} %copy.26), calls=%async_computation.1 | async-start | bytes 8650752 | tf_op jit(solution)/shard_map/all_to_all | solution.py:125
where the time goes:
time: 622 us; the launch traced here: 618 us
  loops' own time  225 us (36%)
  local copies, waits for them, and re-layouts  115 us (18%)
  waiting for transfers between devices  94.4 us (15%)
  other arithmetic  76 us (12%)
  matrix products  61.3 us (10%)
  starting transfers between devices  23 us (4%)
  blocking collectives  21.9 us (4%)
    another operation x1, loops' own time, legendre_table(): lax.scan(recurrence, (zero_state, zero_state, zero_state), jnp.arange(deg...  225 us
    all_to_all x1, waiting for transfers between devices, body(): lax.all_to_all(order_coefs.astype(jnp.bfloat16), 'lat', split_axis=0, con...  94.4 us
    dot_general x1, matrix products, fourier_sums(): jnp.einsum('rmn,jnx->jmrx', fourier_table, grid_data, precision=lax.Preci...  46.7 us
    while x308, other arithmetic  35.7 us
    dynamic_update_slice x44, local copies, waits for them, and re-layouts, legendre_table(): lax.scan(recurrence, (zero_state, zero_state, zero_state), jnp.arange(deg...  29.9 us
    slice x44, local copies, waits for them, and re-layouts, legendre_table(): lax.scan(recurrence, (zero_state, zero_state, zero_state), jnp.arange(deg...  26.9 us
    psum x1, blocking collectives, moments(): first_moment, second_moment = lax.psum((first_moment, second_moment), 'lat')  21.9 us
    all_to_all x1, starting transfers between devices, body(): lax.all_to_all(fourier, 'lat', split_axis=1, concat_axis=0, tiled=True)  16.8 us
  transfers between devices with their start and end apart: 2, of which 1 were waited for; matrix products, arithmetic and copies ran while one was open for 19% of the time, Pallas kernels for 0%

commit v1 on v0

--- a/solution.py
+++ b/solution.py
@@ -7,6 +7,17 @@
 C = 64
 S = 2
 DEG_DEV = 22
+
+
+def cut_along(x, dim, length):
+    before, after = (x.shape[:dim], x.shape[dim + 1 :])
+    return jnp.moveaxis(x.reshape(*before, length, -1, *after), dim, 0)
+
+
+def in_order(pieces, dim):
+    pieces = jnp.moveaxis(pieces, 0, dim)
+    dims = pieces.shape
+    return pieces.reshape(*dims[:dim], dims[dim] * dims[dim + 1], *dims[dim + 2 :])
 
 
 def legendre_table(colatitude, orders, degrees, weight_scale):
@@ -122,9 +133,15 @@
         lax.all_to_all(fourier, "lat", split_axis=1, concat_axis=0, tiled=True),
         preferred_element_type=jnp.float32,
     )
-    coefficients = lax.all_to_all(
-        order_coefs.astype(jnp.bfloat16), "lat", split_axis=0, concat_axis=1, tiled=True
-    )
+    shard = order_coefs.astype(jnp.bfloat16)
+    size, index = (lax.axis_size("lat"), lax.axis_index("lat"))
+    tiles = cut_along(shard, 0, size)
+    finished = [tiles[index]]
+    for lap in range(1, size):
+        sent = tiles[index ^ lap]
+        finished.append(lax.ppermute(sent, "lat", [(i, i ^ lap) for i in range(size)]))
+    tiles = jnp.stack(finished)[index ^ jnp.arange(size)]
+    coefficients = in_order(tiles, 1)
     return apply_filter(coefficients, expanded)
 
 

time: 622 us -> 652 us (1.048)
  local copies, waits for them, and re-layouts: 115 us -> 133 us
  waiting for transfers between devices: 94.4 us -> 82.5 us
  starting transfers between devices: 23 us -> 33.5 us
  loops' own time: 225 us -> 235 us
    all_to_all x1 -> x0, waiting for transfers between devices: 94.4 us -> none  [body(): lax.all_to_all(order_coefs.astype(jnp.bfloat16), 'lat', split_axis=0, con...]
    ppermute x0 -> x15, waiting for transfers between devices: none -> 82.5 us  [body(): lax.ppermute(sent, 'lat', [(i, i ^ lap) for i in range(size)])]
    ppermute x0 -> x15, starting transfers between devices: none -> 16.8 us  [body(): lax.ppermute(sent, 'lat', [(i, i ^ lap) for i in range(size)])]
    another operation x0 -> x2, local copies, waits for them, and re-layouts: none -> 15.2 us  [the longest x1 14.4 us: apply_filter(): coefficients.reshape(coefficients.shape[0], coefficients.shape[1], 2, S, C)]
    unnamed x6 -> x20, local copies, waits for them, and re-layouts: 0.45 us -> 11 us
    another operation x1, loops' own time: 225 us -> 235 us  [legendre_table(): lax.scan(recurrence, (zero_state, zero_state, zero_state), jnp.arange(deg...]
    reshape x1, local copies, waits for them, and re-layouts: 14.4 us -> 6.82 us  [cut_along(): return jnp.moveaxis(x.reshape(*before, length, -1, *after), dim, 0)]
  transfers between devices with their start and end apart: 2 -> 16, of which waited for: 1 -> 11; matrix products, arithmetic and copies ran while one was open for 19% -> 20% of each run, Pallas kernels for 0% -> 0%
where the time goes in v1:
time: 652 us; the launch traced here: 646 us
  loops' own time  235 us (36%)
  local copies, waits for them, and re-layouts  133 us (20%)
  waiting for transfers between devices  82.5 us (13%)
  other arithmetic  76.1 us (12%)
  matrix products  63.3 us (10%)
  starting transfers between devices  33.5 us (5%)
  blocking collectives  21.9 us (3%)
    another operation x1, loops' own time, legendre_table(): lax.scan(recurrence, (zero_state, zero_state, zero_state), jnp.arange(deg...  235 us
    ppermute x15, waiting for transfers between devices, body(): lax.ppermute(sent, 'lat', [(i, i ^ lap) for i in range(size)])  82.5 us
    dot_general x1, matrix products, fourier_sums(): jnp.einsum('rmn,jnx->jmrx', fourier_table, grid_data, precision=lax.Preci...  46.7 us
    while x308, other arithmetic  35.7 us
    dynamic_update_slice x44, local copies, waits for them, and re-layouts, legendre_table(): lax.scan(recurrence, (zero_state, zero_state, zero_state), jnp.arange(deg...  29.8 us
    slice x44, local copies, waits for them, and re-layouts, legendre_table(): lax.scan(recurrence, (zero_state, zero_state, zero_state), jnp.arange(deg...  27.4 us
    psum x1, blocking collectives, moments(): first_moment, second_moment = lax.psum((first_moment, second_moment), 'lat')  21.9 us
    ppermute x15, starting transfers between devices, body(): lax.ppermute(sent, 'lat', [(i, i ^ lap) for i in range(size)])  16.8 us
  transfers between devices with their start and end apart: 16, of which 11 were waited for; matrix products, arithmetic and copies ran while one was open for 20% of the time, Pallas kernels for 0%

profile of v1, /device:TPU:15, one launch (start us, length us, event | category | flops | bytes accessed | tf_op | source)
XLA Modules:
  0.0 646.0 jit_solution(4054847438264490867)
XLA Ops:
  0.6 9.8 %sine_negate_fusion = (f32[1,352,1440]{2,1,0:T(8,128)S(1)}, f32[1,352,1440]{2,1,0:T(8,128)}) fusion(), kind=kLoop, calls=%fused_computation.173 | loop fusion | flops 5068800 | bytes 4055040 | tf_op jit(solution)/shard_map/neg | solution.py:120
  10.5 7.5 %multiply_reduce_fusion.1 = (f32[23,128]{1,0:T(8,128)S(1)}, f32[23,128]{1,0:T(8,128)S(1)}) fusion(f32[23,1440,128]{2,1,0:T(8,128)} %param.5), kind=kLoop, calls=%fused_computation.156 | loop fusion | flops 12712192 | bytes 16980992 | tf_op jit(solution)/shard_map/j,jnx->x/reduce_sum | solution.py:87
  18.4 21.9 %all-reduce = (f32[128]{0:T(128)S(1)}, f32[128]{0:T(128)S(1)}) all-reduce(f32[128]{0:T(128)S(1)} %convolution_bitcast_fusion.1, f32[128]{0:T(128)S(1)} %convolution_bitcast_fusion), channel_id=1, replica_groups=mesh['parts'=2,'lat'=16] {'lat'}, use_global_device_ids=true, to_apply=%region_1.2 | all-reduce | flops 256 | bytes 2048 | tf_op jit(solution)/shard_map/psum | solution.py:90
  40.9 46.7 %convert_bitcast_fusion = bf16[23,352,2,128]{3,1,2,0:T(8,128)(2,1)S(1)} fusion(f32[1,352,1440]{2,1,0:T(8,128)S(1)} %get-tuple-element.529, f32[1,352,1440]{2,1,0:T(8,128)} %get-tuple-element.530, f32[23,1440,128]{2,1,0:T(8,128)} %param.5, f32[128]{0:T(128)S(1)} %get-tuple-element.464, f32[128]{0:T(128)S(1)} %get-tuple-element.465), kind=kOutput, calls=%fused_computation.168 | convolution fusion | flops 35825680384 | bytes 25158656 | tf_op jit(solution)/shard_map/rmn,jnx->jmrx/dot_general | solution.py:99
  87.6 5.1 copy.33
  92.8 7.6 %reshape.419 = bf16[23,352,256]{2,0,1:T(8,128)(2,1)} reshape(bf16[23,352,2,128]{3,2,0,1:T(2,128)(2,1)} %copy.33) | data formatting | bytes 8290304 | tf_op jit(solution)/shard_map/reshape | solution.py:125
  100.4 16.7 %all-to-all-start = ((bf16[23,352,256]{2,0,1:T(8,128)(2,1)}), bf16[23,352,256]{2,0,1:T(8,128)(2,1)}, u32[]{:S(2)}, u32[]{:S(2)}) async-start(bf16[23,352,256]{2,0,1:T(8,128)(2,1)} %reshape.419), calls=%async_computation | async-start | bytes 8650752 | tf_op jit(solution)/shard_map/all_to_all | solution.py:133
  117.3 353.1 %while.23 = (s32[]{:T(128)}, f32[368,22]{0,1:T(8,128)S(1)}, f32[368,22]{0,1:T(8,128)S(1)}, f32[368,22]{0,1:T(8,128)S(1)}, bf16[44,8,368,22]{2,3,1,0:T(8,128)(2,1...) while((s32[]{:T(128)}, f32[368,22]{0,1:T(8,128)S(1)}, ...), condition=%wide.region_6.7_spmd.clone.clone.clone.clone, body=%wide.region_5.6_spmd.clone.clone.clone.clone.sunk | while | flops 2134202 | bytes 2012586 | solution.py:60
  471.2 4.8 copy.24
  476.0 7.0 %all_to_all.16 = bf16[368,22,256]{2,0,1:T(8,128)(2,1)} reshape(bf16[16,23,22,256]{3,1,0,2:T(8,128)(2,1)} %copy.24) | data formatting | bytes 8290304 | tf_op jit(solution)/shard_map/all_to_all | solution.py:133
  483.0 8.2 %convert_bitcast_fusion.1 = bf16[352,22,256]{2,0,1:T(8,128)(2,1)} fusion(bf16[368,22,256]{2,0,1:T(8,128)(2,1)} %all_to_all.16, bf16[352,368,22]{1,2,0:T(8,128)(2,1)} %bitcast.204), kind=kOutput, calls=%fused_computation.169 | convolution fusion | flops 1461075968 | bytes 13809664 | tf_op jit(solution)/shard_map/ljm,jmx->lmx/dot_general | solution.py:130
  491.2 6.8 %reshape.400 = bf16[16,22,22,256]{3,1,0,2:T(8,128)(2,1)} reshape(bf16[352,22,256]{2,0,1:T(8,128)(2,1)} %convert_bitcast_fusion.1) | data formatting | bytes 7929856 | tf_op jit(solution)/shard_map/reshape | solution.py:14
  498.0 3.2 dynamic-slice_bitcast_fusion
  502.2 1.5 collective-permute-start.2
  504.0 1.4 collective-permute-start.4
  505.6 0.7 bitcast_dynamic-update-slice_fusion.15
  506.3 3.6 collective-permute-done.1
  509.9 1.5 collective-permute-start.6
  511.4 0.8 bitcast_dynamic-update-slice_fusion.14
  512.1 4.2 collective-permute-done.2
  516.3 2.1 collective-permute-start.7
  518.4 0.7 bitcast_dynamic-update-slice_fusion.13
  519.4 0.8 bitcast_dynamic-update-slice_fusion.12
  520.1 2.2 collective-permute-start.9
  523.0 10.1 %collective-permute-done.5 = bf16[22,22,256]{2,0,1:T(8,128)(2,1)S(1)} collective-permute-done((bf16[22,22,256]{2,0,1:T(8,128)(2,1)S(1)}, bf16[22,22,256]{2,0,1:T(8,128)(2,1)S(1)}, u32[]{:S(2)}, u32[]{:S(2)}) %collective-permute-start.5) | collective-permute-done | bytes 247840 | tf_op jit(solution)/shard_map/ppermute | solution.py:142
  533.1 4.3 collective-permute-start.10
  537.4 0.8 bitcast_dynamic-update-slice_fusion.10
  538.2 0.8 collective-permute-done.6
  539.4 0.8 bitcast_dynamic-update-slice_fusion.9
  540.1 2.0 collective-permute-start.12
  542.2 0.7 bitcast_dynamic-update-slice_fusion.8
  542.9 22.1 %collective-permute-done.8 = bf16[22,22,256]{2,0,1:T(8,128)(2,1)S(1)} collective-permute-done((bf16[22,22,256]{2,0,1:T(8,128)(2,1)S(1)}, bf16[22,22,256]{2,0,1:T(8,128)(2,1)S(1)}, u32[]{:S(2)}, u32[]{:S(2)}) %collective-permute-start.8) | collective-permute-done | bytes 247840 | tf_op jit(solution)/shard_map/ppermute | solution.py:142
  565.0 0.8 bitcast_dynamic-update-slice_fusion.7
  565.8 10.8 %collective-permute-done.9 = bf16[22,22,256]{2,0,1:T(8,128)(2,1)S(1)} collective-permute-done((bf16[22,22,256]{2,0,1:T(8,128)(2,1)S(1)}, bf16[22,22,256]{2,0,1:T(8,128)(2,1)S(1)}, u32[]{:S(2)}, u32[]{:S(2)}) %collective-permute-start.9) | collective-permute-done | bytes 247840 | tf_op jit(solution)/shard_map/ppermute | solution.py:142
  576.6 0.8 bitcast_dynamic-update-slice_fusion.6
  577.4 5.0 collective-permute-done.10
  582.4 0.8 bitcast_dynamic-update-slice_fusion.5
  583.1 10.9 %collective-permute-done.11 = bf16[22,22,256]{2,0,1:T(8,128)(2,1)S(1)} collective-permute-done((bf16[22,22,256]{2,0,1:T(8,128)(2,1)S(1)}, bf16[22,22,256]{2,0,1:T(8,128)(2,1)S(1)}, u32[]{:S(2)}, u32[]{:S(2)}) %collective-permute-start.11) | collective-permute-done | bytes 247840 | tf_op jit(solution)/shard_map/ppermute | solution.py:142
  594.0 0.8 bitcast_dynamic-update-slice_fusion.4
  594.8 5.6 collective-permute-done.12
  601.1 4.4 collective-permute-done.13
  605.6 0.7 bitcast_dynamic-update-slice_fusion.2
  606.3 5.0 collective-permute-done.14
  611.4 0.7 bitcast_dynamic-update-slice_fusion.1
  612.1 5.0 gather_fusion
  617.1 14.4 %reshape.420 = bf16[22,352,2,2,64]{4,3,2,0,1:T(2,128)(2,1)} reshape(bf16[22,16,22,256]{3,0,2,1:T(8,128)(2,1)} %bitcast.200) | data formatting | bytes 7929856 | tf_op jit(solution)/shard_map/reshape;reshape | solution.py:78
  631.6 8.1 %bitcast_convert_fusion = bf16[22,2,64,352,2]{3,2,4,1,0:T(8,128)(2,1)} fusion(bf16[22,352,2,2,64,1]{4,3,2,0,1,5:T(2,128)(2,1)} %bitcast.199, bf16[22,1,64,2,64]{2,4,1,3,0:T(8,128)(2,1)S(1)} %get-tuple-element.528, bf16[22,1,64,2,64]{2,4,1,3,0:T(8,128)(2,1)S(1)} %get-tuple-element.527), kind=kOutput, calls=%fused_computation.158 | convolution fusion | flops 510935040 | bytes 8650752 | tf_op jit(solution)/shard_map/lmrsc,lrcqo->lmqso/dot_general | solution.py:79
  639.7 6.3 copy.28
  (1360 shorter events, 123.4 us)
Async XLA Ops:
  10.5 7.9 %copy-start.1 = (f32[64]{0:T(128)S(1)}, f32[64]{0:T(128)}, u32[]{:S(2)}) copy-start(f32[64]{0:T(128)} %param.6) | copy-start | bytes 772
  100.4 370.8 %all-to-all-start = ((bf16[23,352,256]{2,0,1:T(8,128)(2,1)}), bf16[23,352,256]{2,0,1:T(8,128)(2,1)}, u32[]{:S(2)}, u32[]{:S(2)}) async-start(bf16[23,352,256]{2,0,1:T(8,128)(2,1)} %reshape.419), calls=%async_computation | async-start | bytes 8650752 | tf_op jit(solution)/shard_map/all_to_all | solution.py:133
  117.3 353.2 %copy-start = (bf16[22,2,64,64]{3,2,1,0:T(8,128)(2,1)S(1)}, bf16[22,2,64,64]{3,2,1,0:T(8,128)(2,1)}, u32[]{:S(2)}) copy-start(bf16[22,2,64,64]{3,2,1,0:T(8,128)(2,1)} %param.7) | copy-start | bytes 1081348
  501.3 4.2 collective-permute-start
  501.9 8.0 %collective-permute-start.1 = (bf16[22,22,256]{2,0,1:T(8,128)(2,1)S(1)}, bf16[22,22,256]{2,0,1:T(8,128)(2,1)S(1)}, u32[]{:S(2)}, u32[]{:S(2)}) collective-permute-start(bf16[22,22,256]{2,0,1:T(8,128)(2,1)S(1)} %get-tuple-element.522), channel_id=1, source_target_pairs={{0,2},{1,3},{2,0},{3,1},{4,6},{5,7},{6,4},{7,5},{8,10},{9,11},{10,... | collective-permute-start | bytes 743432 | tf_op jit(solution)/shard_map/ppermute | solution.py:142
  502.2 14.0 %collective-permute-start.2 = (bf16[22,22,256]{2,0,1:T(8,128)(2,1)S(1)}, bf16[22,22,256]{2,0,1:T(8,128)(2,1)S(1)}, u32[]{:S(2)}, u32[]{:S(2)}) collective-permute-start(bf16[22,22,256]{2,0,1:T(8,128)(2,1)S(1)} %get-tuple-element.521), channel_id=1, source_target_pairs={{0,3},{1,2},{2,1},{3,0},{4,7},{5,6},{6,5},{7,4},{8,11},{9,10},{10,... | collective-permute-start | bytes 743432 | tf_op jit(solution)/shard_map/ppermute | solution.py:142
  503.8 15.4 %collective-permute-start.3 = (bf16[22,22,256]{2,0,1:T(8,128)(2,1)S(1)}, bf16[22,22,256]{2,0,1:T(8,128)(2,1)S(1)}, u32[]{:S(2)}, u32[]{:S(2)}) collective-permute-start(bf16[22,22,256]{2,0,1:T(8,128)(2,1)S(1)} %get-tuple-element.520), channel_id=1, source_target_pairs={{0,4},{1,5},{2,6},{3,7},{4,0},{5,1},{6,2},{7,3},{8,12},{9,13},{10,... | collective-permute-start | bytes 743432 | tf_op jit(solution)/shard_map/ppermute | solution.py:142
  504.0 16.1 %collective-permute-start.4 = (bf16[22,22,256]{2,0,1:T(8,128)(2,1)S(1)}, bf16[22,22,256]{2,0,1:T(8,128)(2,1)S(1)}, u32[]{:S(2)}, u32[]{:S(2)}) collective-permute-start(bf16[22,22,256]{2,0,1:T(8,128)(2,1)S(1)} %get-tuple-element.519), channel_id=1, source_target_pairs={{0,5},{1,4},{2,7},{3,6},{4,1},{5,0},{6,3},{7,2},{8,13},{9,12},{10,... | collective-permute-start | bytes 743432 | tf_op jit(solution)/shard_map/ppermute | solution.py:142
  505.5 27.7 %collective-permute-start.5 = (bf16[22,22,256]{2,0,1:T(8,128)(2,1)S(1)}, bf16[22,22,256]{2,0,1:T(8,128)(2,1)S(1)}, u32[]{:S(2)}, u32[]{:S(2)}) collective-permute-start(bf16[22,22,256]{2,0,1:T(8,128)(2,1)S(1)} %get-tuple-element.518), channel_id=1, source_target_pairs={{0,6},{1,7},{2,4},{3,5},{4,2},{5,3},{6,0},{7,1},{8,14},{9,15},{10,... | collective-permute-start | bytes 743432 | tf_op jit(solution)/shard_map/ppermute | solution.py:142
  509.9 29.0 %collective-permute-start.6 = (bf16[22,22,256]{2,0,1:T(8,128)(2,1)S(1)}, bf16[22,22,256]{2,0,1:T(8,128)(2,1)S(1)}, u32[]{:S(2)}, u32[]{:S(2)}) collective-permute-start(bf16[22,22,256]{2,0,1:T(8,128)(2,1)S(1)} %get-tuple-element.517), channel_id=1, source_target_pairs={{0,7},{1,6},{2,5},{3,4},{4,3},{5,2},{6,1},{7,0},{8,15},{9,14},{10,... | collective-permute-start | bytes 743432 | tf_op jit(solution)/shard_map/ppermute | solution.py:142
  516.3 23.9 %collective-permute-start.7 = (bf16[22,22,256]{2,0,1:T(8,128)(2,1)S(1)}, bf16[22,22,256]{2,0,1:T(8,128)(2,1)S(1)}, u32[]{:S(2)}, u32[]{:S(2)}) collective-permute-start(bf16[22,22,256]{2,0,1:T(8,128)(2,1)S(1)} %get-tuple-element.516), channel_id=1, source_target_pairs={{0,8},{1,9},{2,10},{3,11},{4,12},{5,13},{6,14},{7,15},{8,0},{9,1},... | collective-permute-start | bytes 743432 | tf_op jit(solution)/shard_map/ppermute | solution.py:142
  519.1 45.9 %collective-permute-start.8 = (bf16[22,22,256]{2,0,1:T(8,128)(2,1)S(1)}, bf16[22,22,256]{2,0,1:T(8,128)(2,1)S(1)}, u32[]{:S(2)}, u32[]{:S(2)}) collective-permute-start(bf16[22,22,256]{2,0,1:T(8,128)(2,1)S(1)} %get-tuple-element.515), channel_id=1, source_target_pairs={{0,9},{1,8},{2,11},{3,10},{4,13},{5,12},{6,15},{7,14},{8,1},{9,0},... | collective-permute-start | bytes 743432 | tf_op jit(solution)/shard_map/ppermute | solution.py:142
  520.1 56.5 %collective-permute-start.9 = (bf16[22,22,256]{2,0,1:T(8,128)(2,1)S(1)}, bf16[22,22,256]{2,0,1:T(8,128)(2,1)S(1)}, u32[]{:S(2)}, u32[]{:S(2)}) collective-permute-start(bf16[22,22,256]{2,0,1:T(8,128)(2,1)S(1)} %get-tuple-element.514), channel_id=1, source_target_pairs={{0,10},{1,11},{2,8},{3,9},{4,14},{5,15},{6,12},{7,13},{8,2},{9,3},... | collective-permute-start | bytes 743432 | tf_op jit(solution)/shard_map/ppermute | solution.py:142
  533.1 49.2 %collective-permute-start.10 = (bf16[22,22,256]{2,0,1:T(8,128)(2,1)S(1)}, bf16[22,22,256]{2,0,1:T(8,128)(2,1)S(1)}, u32[]{:S(2)}, u32[]{:S(2)}) collective-permute-start(bf16[22,22,256]{2,0,1:T(8,128)(2,1)S(1)} %get-tuple-element.513), channel_id=1, source_target_pairs={{0,11},{1,10},{2,9},{3,8},{4,15},{5,14},{6,13},{7,12},{8,3},{9,2},... | collective-permute-start | bytes 743432 | tf_op jit(solution)/shard_map/ppermute | solution.py:142
  538.9 55.1 %collective-permute-start.11 = (bf16[22,22,256]{2,0,1:T(8,128)(2,1)S(1)}, bf16[22,22,256]{2,0,1:T(8,128)(2,1)S(1)}, u32[]{:S(2)}, u32[]{:S(2)}) collective-permute-start(bf16[22,22,256]{2,0,1:T(8,128)(2,1)S(1)} %get-tuple-element.512), channel_id=1, source_target_pairs={{0,12},{1,13},{2,14},{3,15},{4,8},{5,9},{6,10},{7,11},{8,4},{9,5},... | collective-permute-start | bytes 743432 | tf_op jit(solution)/shard_map/ppermute | solution.py:142
  540.1 60.2 %collective-permute-start.12 = (bf16[22,22,256]{2,0,1:T(8,128)(2,1)S(1)}, bf16[22,22,256]{2,0,1:T(8,128)(2,1)S(1)}, u32[]{:S(2)}, u32[]{:S(2)}) collective-permute-start(bf16[22,22,256]{2,0,1:T(8,128)(2,1)S(1)} %get-tuple-element.511), channel_id=1, source_target_pairs={{0,13},{1,12},{2,15},{3,14},{4,9},{5,8},{6,11},{7,10},{8,5},{9,4},... | collective-permute-start | bytes 743432 | tf_op jit(solution)/shard_map/ppermute | solution.py:142
  565.0 40.6 %collective-permute-start.13 = (bf16[22,22,256]{2,0,1:T(8,128)(2,1)S(1)}, bf16[22,22,256]{2,0,1:T(8,128)(2,1)S(1)}, u32[]{:S(2)}, u32[]{:S(2)}) collective-permute-start(bf16[22,22,256]{2,0,1:T(8,128)(2,1)S(1)} %get-tuple-element.510), channel_id=1, source_target_pairs={{0,14},{1,15},{2,12},{3,13},{4,10},{5,11},{6,8},{7,9},{8,6},{9,7},... | collective-permute-start | bytes 743432 | tf_op jit(solution)/shard_map/ppermute | solution.py:142
  576.6 34.8 %collective-permute-start.14 = (bf16[22,22,256]{2,0,1:T(8,128)(2,1)S(1)}, bf16[22,22,256]{2,0,1:T(8,128)(2,1)S(1)}, u32[]{:S(2)}, u32[]{:S(2)}) collective-permute-start(bf16[22,22,256]{2,0,1:T(8,128)(2,1)S(1)} %get-tuple-element.509), channel_id=1, source_target_pairs={{0,15},{1,14},{2,13},{3,12},{4,11},{5,10},{6,9},{7,8},{8,7},{9,6},... | collective-permute-start | bytes 743432 | tf_op jit(solution)/shard_map/ppermute | solution.py:142
